TPU v7x, 1024 devices: a whole 4x4x32 slice. The times are simulated.
1024 devices in a mesh: dom: 64 (over z_lo, y), sub: 16 (over x, z_hi, core).
Axes of the slice: x: 4, y: 4, z: 32 (z_hi: 2, z_lo: 16; z = z_hi * 16 + z_lo), core: 2. Of those that a mesh axis runs over, the one named last changes fastest.
Arguments:
- excitation: bfloat16 [64, 512, 4096], P('dom', None, 'sub'), may hold values from -6 to 6
- stiffness: float32 [64, 512, 512], P('dom'), may hold values from -2 to 14, as said below
- traces_prev: float32 [64, 32768], P('dom', 'sub'), may hold values from -6 to 6
- neighbours: int32 [64, 4], P('dom'), may hold values from 0 to 63, as said below
- far_list: int32 [64, 2], P('dom'), may hold values from 0 to 63, as said below
- face_perm: int32 [64, 4, 128], P('dom'), may hold values from 0 to 127, each once within a row
- live_columns: int32 [64], P('dom'), may hold values from 2048 to 4096, as said below
- far_block: bfloat16 [64, 2, 192, 32768], P('dom', None, None, 'sub'), may hold values from -0.03125 to 0.03125
- in_basis: bfloat16 [64, 192, 32768], P('dom', 'sub'), may hold values from -0.4375 to 0.4375
Outputs:
- field: float32 [64, 512, 4096], P('dom', None, 'sub')
- traces_next: float32 [64, 32768], P('dom', 'sub')
Inputs may be any that keep to these rules, and one draw needn't show every extreme that they name: `neighbours`: row d names 4 distinct domains other than d; e names d whenever d names e, and each column names every domain once. `far_list`: row d names 2 distinct domains, neither d nor any in row d of neighbours; each column names every domain once. `live_columns`: some domain uses all 4096 columns and some uses exactly half of them. `stiffness`: symmetric in its last two dimensions.
All inputs are finite; a program needn't handle non-finite values.
Results may differ from a plain program's by a relative error of at most 0.0022.
Values may be sent and summed in bfloat16 or wider, within the bound.
A program may use at most 64 MiB of HBM per device.

v0:
```python
import jax
import jax.numpy as jnp
from jax import lax
from jax.sharding import PartitionSpec as P

BLK = 512
TROW = 8
NB = 4
DEG = 8
PATCH = 128


cheb_lower = 0.8
cheb_upper = 24.0
robin_gain = 2.0


def apply_operator(stiff_block, vectors):
    row_index = lax.broadcasted_iota(jnp.int32, vectors.shape, 0)
    boundary = jnp.where(row_index < TROW, robin_gain * vectors, jnp.zeros_like(vectors))
    product = jnp.dot(
        stiff_block, vectors, precision=lax.Precision.HIGHEST, preferred_element_type=jnp.float32
    )
    return product + boundary


def chebyshev_smooth(stiff_block, source):
    centre_value = 0.5 * (cheb_upper + cheb_lower)
    half_width = 0.5 * (cheb_upper - cheb_lower)
    sigma_ratio = centre_value / half_width
    rho_previous = 1.0 / sigma_ratio
    solution = jnp.zeros_like(source)
    residue = source
    update = source / centre_value
    for degree_step in range(DEG):
        solution = solution + update
        if degree_step + 1 < DEG:
            residue = residue - apply_operator(stiff_block, update)
            rho_next = 1.0 / (2.0 * sigma_ratio - rho_previous)
            update = rho_next * rho_previous * update + 2.0 * rho_next / half_width * residue
            rho_previous = rho_next
    return solution


def body(
    excitation,
    stiffness,
    traces_prev,
    neighbours,
    far_list,
    face_perm,
    live_columns,
    far_block,
    in_basis,
):
    trace_len = traces_prev.shape[1]
    col_count = excitation.shape[2]
    gathered = lax.all_gather(traces_prev, "dom", axis=0, tiled=True)
    near_rows = jnp.take(gathered, neighbours[0], axis=0)
    near_patch = near_rows.reshape(NB, trace_len // PATCH, PATCH)
    patch_index = lax.broadcasted_iota(jnp.int32, (NB, PATCH, PATCH), 1)
    selector = (face_perm[0][:, None, :] == patch_index).astype(jnp.float32)
    near_sum = jnp.einsum(
        "jqp,jpk->qk", near_patch, selector, precision=lax.Precision.HIGHEST
    ).reshape(trace_len)
    far_rows = jnp.take(gathered, far_list[0], axis=0).astype(jnp.bfloat16)
    partial_coef = jnp.einsum(
        "frk,fk->r", far_block[0], far_rows, preferred_element_type=jnp.float32
    )
    coef_share = lax.psum_scatter(partial_coef, "sub", scatter_dimension=0, tiled=True).astype(
        jnp.bfloat16
    )
    basis_cols = in_basis[0]
    far_sum = lax.psum_scatter(
        jnp.dot(coef_share, basis_cols, preferred_element_type=jnp.float32),
        "sub",
        scatter_dimension=0,
        tiled=True,
    )
    incoming = (near_sum + far_sum).reshape(col_count, TROW).T
    columns = lax.axis_index("sub") * col_count + lax.broadcasted_iota(jnp.int32, (1, col_count), 1)
    live_mask = columns < live_columns[0]
    stiff_block = stiffness[0]
    source = excitation[0].astype(jnp.float32) + jnp.pad(incoming, ((0, BLK - TROW), (0, 0)))
    source = jnp.where(live_mask, source, jnp.zeros_like(source))
    field_values = chebyshev_smooth(stiff_block, source)
    outgoing = 2.0 * robin_gain * field_values[:TROW] - incoming
    outgoing = jnp.where(live_mask, outgoing, jnp.zeros_like(outgoing))
    return (field_values[None], outgoing.T.reshape(1, trace_len))


def solution(mesh):
    placed = (
        P("dom", None, "sub"),
        P("dom", None, None),
        P("dom", "sub"),
        P("dom", None),
        P("dom", None),
        P("dom", None, None),
        P("dom"),
        P("dom", None, None, "sub"),
        P("dom", "sub", None),
    )
    return jax.shard_map(
        body,
        mesh=mesh,
        in_specs=placed,
        out_specs=(P("dom", None, "sub"), P("dom", "sub")),
        check_vma=False,
    )
```

profile of v0, /device:TPU:1, one launch (start us, length us, event | category | flops | bytes accessed | tf_op | source)
XLA Modules:
  0.0 930.6 jit_solution(17181905768654130186)
XLA Ops:
  7.2 0.0 copy-start
  7.2 0.0 all-reduce.5.cloned.1.call-start
  7.2 0.8 fusion.59
  8.0 0.7 compare_and_fusion
  8.7 378.7 %all-gather = f32[64,1,2048]{2,1,0:T(1,128)S(1)} all-gather(f32[1,1,2048]{2,1,0:T(1,128)} %bitcast.147), channel_id=1, replica_groups=mesh['dom'=64,'sub'=16] {'dom'}, dimensions={0}, use_global_device_ids=true | all-gather | bytes 532480 | tf_op jit(solution)/shard_map/all_gather | solution.py:58
  387.4 0.2 copy.27
  387.5 0.0 copy-start.5
  387.5 0.0 copy-start.2
  387.5 0.6 gather_fusion.1
  388.1 0.1 fusion.57
  388.2 0.0 copy-done
  388.2 0.5 fusion
  388.7 128.3 %all-reduce.1 = bf16[192]{0:T(256)(128)(2,1)S(1)} all-reduce(f32[192]{0:T(256)S(1)} %bitcast.148), channel_id=2, replica_groups=mesh['dom'=64,'sub'=16] {'sub'}, use_global_device_ids=true, to_apply=%region_0.1.clone | all-reduce | flops 192 | bytes 1152
  517.0 1.3 dynamic-slice
  518.9 2.2 fusion.27
  521.1 0.0 all-reduce.5.cloned.1.call-update
  522.5 0.0 copy-done.2
  522.5 0.8 copy.15
  523.4 0.6 gather_fusion
  524.0 386.8 %all-reduce.5.cloned.1.call-done = f32[32768]{0:T(1024)} async-done(((f32[32768]{0:T(1024)}), f32[32768]{0:T(1024)}) %all-reduce.5.cloned.1.call-update) | async-done | bytes 131088
  910.8 0.9 fusion.19
  911.7 0.1 reshape.98
  911.8 2.2 fusion.15
  914.0 1.2 fusion.13
  915.3 1.4 multiply_add_fusion.2
  916.7 1.1 fusion.9
  917.8 1.1 fusion.7
  918.9 1.3 fusion.5
  920.2 1.7 fusion.18
  921.9 0.1 fusion.51
  922.0 0.7 reshape.99
  922.8 1.0 copy.16
  (13 shorter events, 0.0 us)
Async XLA Ops:
  7.2 381.0 %copy-start = (bf16[1,2,192,2048]{3,2,1,0:T(8,128)(2,1)S(1)}, bf16[1,2,192,2048]{3,2,1,0:T(8,128)(2,1)}, u32[]{:S(2)}) copy-start(bf16[1,2,192,2048]{3,2,1,0:T(8,128)(2,1)} %param.16) | copy-start | bytes 4718596
  7.2 903.6 %all-reduce.5.cloned.1.call-start = ((), (), s32[]{:S(2)}) async-start(), calls=%async_computation | async-start | bytes 262144
  387.5 133.6 %copy-start.5 = (s32[1,4]{1,0:T(1,128)S(1)}, s32[1,4]{1,0:T(1,128)}, u32[]{:S(2)}) copy-start(s32[1,4]{1,0:T(1,128)} %param.12) | copy-start | bytes 52
  387.5 135.0 %copy-start.2 = (bf16[1,512,256]{2,1,0:T(8,128)(2,1)S(1)}, bf16[1,512,256]{2,1,0:T(8,128)(2,1)}, u32[]{:S(2)}) copy-start(bf16[1,512,256]{2,1,0:T(8,128)(2,1)} %param.9) | copy-start | bytes 786436
  388.2 522.6 %copy-start.4 = (s32[1,4,128]{2,1,0:T(4,128)S(1)}, s32[1,4,128]{2,1,0:T(4,128)}, u32[]{:S(2)}) copy-start(s32[1,4,128]{2,1,0:T(4,128)} %param.14) | copy-start | bytes 6148
  388.7 523.1 %copy-start.1 = (f32[1,512,512]{2,1,0:T(8,128)S(1)}, f32[1,512,512]{2,1,0:T(8,128)}, u32[]{:S(2)}) copy-start(f32[1,512,512]{2,1,0:T(8,128)} %param.10) | copy-start | bytes 3145732
  523.4 390.7 %copy-start.3 = (bf16[1,512,256]{1,2,0:T(8,128)(2,1)S(1)}, bf16[1,512,256]{1,2,0:T(8,128)(2,1)}, u32[]{:S(2)}) copy-start(bf16[1,512,256]{1,2,0:T(8,128)(2,1)} %copy.15) | copy-start | bytes 786436
Sparse Core Ops, SparseCore 0:
  521.3 389.4 all-reduce.4
where the time goes:
time: 931 us
  blocking collectives  507 us (54%)
  waiting for transfers between devices  387 us (42%)
  between operations  16.2 us (2%)
  matrix products  13.7 us (1%)
    unnamed x2, waiting for transfers between devices  387 us
    all_gather x1, blocking collectives, body(): gathered = lax.all_gather(traces_prev, 'dom', axis=0, tiled=True)  379 us
    unnamed x1, blocking collectives  128 us
  transfers between devices with their start and end apart: 1, of which 1 were waited for; matrix products, arithmetic and copies ran while one was open for 0% of the time, Pallas kernels for 0%

commit v1 on v0

v1 whole, which is shorter than its diff:
```python
import functools
import jax
import jax.numpy as jnp
from jax import lax
from jax.experimental import pallas as pl
from jax.experimental.pallas import tpu as pltpu
from jax.sharding import PartitionSpec as P

MESH = pl.DeviceIdType.MESH
F32 = jnp.float32
BF16 = jnp.bfloat16

BLK = 512
TROW = 8
NB = 4
FAR = 2
DEG = 8
PATCH = 128
RANK = 192
ZN, YN, XN = 16, 4, 4
SUB = 16
OWN = RANK // SUB
QN = 16
COLS = 256
VCOLS = COLS + PATCH

cheb_lower = 0.8
cheb_upper = 24.0
robin_gain = 2.0


def cheb_constants():
    centre = 0.5 * (cheb_upper + cheb_lower)
    half = 0.5 * (cheb_upper - cheb_lower)
    ratio = centre / half
    previous = 1.0 / ratio
    steps = []
    for _ in range(DEG - 1):
        following = 1.0 / (2.0 * ratio - previous)
        steps.append((following * previous, 2.0 * following / half))
        previous = following
    return centre, steps


def split2(values):
    high = values.astype(BF16)
    low = (values - high.astype(F32)).astype(BF16)
    return high, low


def split3(values):
    high = values.astype(BF16)
    rest = values - high.astype(F32)
    middle = rest.astype(BF16)
    low = (rest - middle.astype(F32)).astype(BF16)
    return high, middle, low


def dot_nt(left, right):
    return lax.dot_general(left, right, (((1,), (1,)), ((), ())), preferred_element_type=F32)


def iota(shape, axis):
    return lax.broadcasted_iota(jnp.int32, shape, axis)


def kernel(
    coef_ref,
    exc_hbm,
    stiff_hbm,
    trace_ref,
    neigh_ref,
    farl_ref,
    perm_ref,
    live_ref,
    far_hbm,
    basis_hbm,
    field_ref,
    next_ref,
    exc_v,
    stiff_v,
    far_v,
    basis_v,
    basis_d,
    a3,
    u_v,
    r_v,
    x_v,
    own_t,
    rows_v,
    tab_v,
    sel_v,
    fsend,
    frecv,
    nsend,
    nrecv,
    csend,
    crecv,
    psend,
    precv,
    hsend,
    hrecv,
    t0_v,
    g3_v,
    b3_v,
    lsem,
    zs,
    zr,
    ts,
    tr,
    fs,
    fr,
    ns,
    nr,
    cs,
    cr,
    ps,
    pr,
    hs,
    hr,
):
    dom = lax.axis_index("dom")
    sub = lax.axis_index("sub")
    z, y = dom // YN, dom % YN
    x, h, c = sub // 4, (sub // 2) % 2, sub % 2
    s8 = x * 2 + c

    def z_peer(k):
        return (((z + k) % ZN) * YN + y, sub)

    def y_peer(k):
        return (z * YN + (y + k) % YN, sub)

    def s_peer(k):
        return (dom, (sub + k) % SUB)

    def e_peer(k):
        t = (s8 + k) % 8
        return (dom, (t // 2) * 4 + h * 2 + t % 2)

    across = (dom, x * 4 + (1 - h) * 2 + c)

    barrier = pltpu.get_barrier_semaphore()
    peers = [z_peer(k) for k in range(1, ZN)] + [y_peer(k) for k in range(1, YN)]
    peers += [s_peer(k) for k in range(1, SUB)]
    for peer in peers:
        pl.semaphore_signal(barrier, inc=1, device_id=peer, device_id_type=MESH)

    loads = [
        pltpu.make_async_copy(stiff_hbm, stiff_v, lsem.at[0]),
        pltpu.make_async_copy(exc_hbm, exc_v, lsem.at[1]),
        pltpu.make_async_copy(basis_hbm, basis_v, lsem.at[2]),
        pltpu.make_async_copy(far_hbm, far_v, lsem.at[3]),
    ]
    for load in loads:
        load.start()

    for q in range(QN):
        own_t[q : q + 1, :] = trace_ref[:, q * PATCH : (q + 1) * PATCH]
    rows_v[z] = own_t[...]
    tab_v[0, 0:4, :] = perm_ref[0]
    for j in range(NB):
        tab_v[0, 4 + j : 5 + j, :] = jnp.full((1, PATCH), neigh_ref[0, j], jnp.int32)
    for f in range(FAR):
        tab_v[0, 8 + f : 9 + f, :] = jnp.full((1, PATCH), farl_ref[0, f], jnp.int32)
    tab_v[0, 10:16, :] = jnp.zeros((6, PATCH), jnp.int32)

    loads[0].wait()
    row = iota((BLK, BLK), 0)
    col = iota((BLK, BLK), 1)
    operator = stiff_v[0] + jnp.where((row == col) & (row < TROW), robin_gain, 0.0)
    a_high, a_low = split2(operator)
    a3[:, 0:BLK] = a_high
    a3[:, BLK : 2 * BLK] = a_low
    a3[:, 2 * BLK : 3 * BLK] = a_high

    live = live_ref[0]
    loads[1].wait()
    column = sub * COLS + iota((BLK, COLS), 1)
    r_v[:, 0:COLS] = jnp.where(column < live, exc_v[0].astype(F32), 0.0)
    r_v[:, COLS:] = jnp.where(iota((BLK, PATCH), 0) == iota((BLK, PATCH), 1) % TROW, 1.0, 0.0)
    centre, _ = cheb_constants()
    first = r_v[...] * (1.0 / centre)
    u_v[...] = first
    x_v[...] = first

    def smooth(step, carry):
        u_high, u_low = split2(u_v[...])
        moved = jnp.dot(
            a3[...],
            jnp.concatenate([u_high, u_high, u_low], axis=0),
            preferred_element_type=F32,
        )
        res = r_v[...] - moved
        r_v[...] = res
        following = coef_ref[step, 0] * u_v[...] + coef_ref[step, 1] * res
        u_v[...] = following
        x_v[...] += following
        return carry

    lax.fori_loop(0, 4, smooth, 0)

    pl.semaphore_wait(barrier, len(peers))

    def remote(src, dst, send, recv, peer):
        return pltpu.make_async_remote_copy(
            src_ref=src,
            dst_ref=dst,
            send_sem=send,
            recv_sem=recv,
            device_id=peer,
            device_id_type=MESH,
        )

    z_copies = [
        remote(own_t, rows_v.at[z], zs.at[k], zr.at[k], z_peer(k)) for k in range(1, ZN)
    ]
    t_copies = [
        remote(tab_v.at[0], tab_v.at[YN - k], ts.at[k], tr.at[k], y_peer(k)) for k in range(1, YN)
    ]
    for copy in z_copies:
        copy.start()
    for copy in t_copies:
        copy.start()

    lax.fori_loop(4, DEG - 1, smooth, 0)

    loads[2].wait()
    for r in range(OWN):
        basis_d[r] = basis_v[0, r : r + 1, :].astype(F32).reshape(256, PATCH)

    lane = iota((PATCH, PATCH), 1)
    sublane = iota((PATCH, PATCH), 0)
    g_high, g_low = split2(x_v[:, COLS:])
    g3_v[:, 0:PATCH] = g_high
    g3_v[:, PATCH : 2 * PATCH] = g_high
    g3_v[:, 2 * PATCH :] = g_low
    tiled = jnp.concatenate([x_v[0:TROW, COLS:]] * QN, axis=0)
    gain = jnp.where(lane // TROW == sublane // TROW, (2.0 * robin_gain) * tiled, 0.0)
    b_high, b_low = split2(gain)
    b3_v[:, 0:PATCH] = b_high
    b3_v[:, PATCH : 2 * PATCH] = b_high
    b3_v[:, 2 * PATCH :] = b_low

    pieces = split3((2.0 * robin_gain) * x_v[0:TROW, 0:COLS])
    stacked = jnp.concatenate([piece.astype(F32) for piece in pieces], axis=0).astype(BF16)
    spread = iota((COLS, PATCH), 1) // TROW
    place = iota((COLS, PATCH), 0)
    keep = iota((TROW, PATCH), 0) == iota((TROW, PATCH), 1) % TROW
    for q in range(QN):
        pick = jnp.where(place == q * 16 + spread, 1.0, 0.0).astype(BF16)
        got = jnp.dot(stacked, pick, preferred_element_type=F32)
        got = got[0:8] + got[8:16] + got[16:24]
        t0_v[q : q + 1, :] = jnp.sum(jnp.where(keep, got, 0.0), axis=0, keepdims=True)

    for copy in t_copies:
        copy.wait_recv()
    for t in range(YN):
        for j in range(NB):
            hit = tab_v[t, j : j + 1, :] == sublane
            sel_v[t, j * PATCH : (j + 1) * PATCH, :] = jnp.where(hit, 1.0, 0.0).astype(BF16)

    loads[3].wait()
    for copy in z_copies:
        copy.wait_recv()

    def pick_row(t, entry):
        wanted = jnp.broadcast_to(tab_v[t, entry : entry + 1, :], (QN, PATCH))
        found = jnp.zeros((QN, PATCH), F32)
        for k in range(ZN):
            found = jnp.where(wanted == k * YN + y, rows_v[k], found)
        return found

    f_copies = []
    for t in (2, 1, 3, 0):
        for f in range(FAR):
            fsend[t, f] = pick_row(t, 8 + f)
        if t:
            copy = remote(fsend.at[t], frecv.at[t], fs.at[t], fr.at[t], y_peer(t))
            copy.start()
            f_copies.append(copy)
    n_copies = []
    for t in (2, 1, 3, 0):
        faces = jnp.concatenate([pick_row(t, 4 + j) for j in range(NB)], axis=1)
        three = split3(faces)
        got = jnp.dot(
            jnp.concatenate(three, axis=0), sel_v[t], preferred_element_type=F32
        )
        nsend[t] = (got[0:QN] + got[QN : 2 * QN]) + got[2 * QN :]
        if t:
            copy = remote(nsend.at[t], nrecv.at[t], ns.at[t], nr.at[t], y_peer(t))
            copy.start()
            n_copies.append(copy)

    for copy in f_copies:
        copy.wait_recv()
    partial = jnp.zeros((8, RANK), F32)
    for f in range(FAR):
        remote_rows = ((fsend[0, f] + frecv[1, f]) + (frecv[2, f] + frecv[3, f])).astype(BF16).astype(F32)
        flat = jnp.concatenate([remote_rows[q : q + 1, :] for q in range(QN)], axis=1)
        flat = jnp.broadcast_to(flat, (8, QN * PATCH)).astype(BF16)
        partial += dot_nt(flat, far_v[0, f])
    csend[:, 0:RANK] = partial[0:1, :]
    csend[:, RANK:] = jnp.zeros((1, 256 - RANK), F32)
    crecv[0] = csend[...]
    c_copies = [
        remote(csend, crecv.at[k], cs.at[k], cr.at[k], s_peer(k)) for k in range(1, SUB)
    ]
    for copy in c_copies:
        copy.start()
    for copy in c_copies:
        copy.wait_recv()

    total = crecv[0]
    for k in range(1, SUB):
        total += crecv[k]
    total = total.astype(BF16).astype(F32)
    mine = iota((16, 256), 1) == sub * OWN + iota((16, 256), 0)
    shares = jnp.sum(jnp.where(mine, jnp.broadcast_to(total, (16, 256)), 0.0), axis=1, keepdims=True)
    weights = [jnp.broadcast_to(shares[r : r + 1, :], (QN, PATCH)) for r in range(OWN)]
    for xx in range(XN):
        for hh in range(2):
            for cc in range(2):
                at = (xx * 4 + hh * 2 + cc) * QN
                value = weights[0] * basis_d[0, at : at + QN, :]
                for r in range(1, OWN):
                    value += weights[r] * basis_d[r, at : at + QN, :]
                psend[hh, xx * 2 + cc] = value
    p_copies = [[], []]
    for g in range(2):
        half = 1 - h if g == 0 else h
        for k in range(1, 8):
            copy = remote(
                psend.at[half, (s8 + k) % 8],
                precv.at[g, k],
                ps.at[g, k],
                pr.at[g, k],
                e_peer(k),
            )
            copy.start()
            p_copies[g].append(copy)
    for copy in p_copies[0]:
        copy.wait_recv()
    other = psend[1 - h, s8]
    for k in range(1, 8):
        other += precv[0, k]
    hsend[...] = other
    h_copy = remote(hsend, hrecv, hs.at[0], hr.at[0], across)
    h_copy.start()

    for copy in n_copies:
        copy.wait_recv()
    near = (nsend[0] + nrecv[1]) + (nrecv[2] + nrecv[3])
    for copy in p_copies[1]:
        copy.wait_recv()
    far = psend[h, s8]
    for k in range(1, 8):
        far += precv[1, k]
    h_copy.wait_recv()
    incoming = near + (far + hrecv[...])

    patch_col = sub * COLS + iota((QN, PATCH), 0) * 16 + iota((QN, PATCH), 1) // TROW
    live_trace = patch_col < live
    incoming = jnp.where(live_trace, incoming, 0.0)
    i_high, i_low = split2(incoming)
    i3 = jnp.concatenate([i_high, i_low, i_high], axis=1)
    outgoing = t0_v[...] + dot_nt(i3, b3_v[...]) - incoming
    outgoing = jnp.where(live_trace, outgoing, 0.0)
    for q in range(QN):
        next_ref[:, q * PATCH : (q + 1) * PATCH] = outgoing[q : q + 1, :]

    lanes3 = (iota((16, 3 * PATCH), 1) % PATCH) // TROW == iota((16, 3 * PATCH), 0)
    i3f = i3.astype(F32)
    wide = jnp.concatenate(
        [
            jnp.where(lanes3, jnp.broadcast_to(i3f[q : q + 1, :], (16, 3 * PATCH)), 0.0)
            for q in range(QN)
        ],
        axis=0,
    ).astype(BF16)
    field_ref[0] = x_v[:, 0:COLS] + dot_nt(g3_v[...], wide)

    for copy in z_copies + t_copies + f_copies + n_copies + c_copies + p_copies[0] + p_copies[1]:
        copy.wait_send()
    h_copy.wait_send()


def body(*operands):
    _, steps = cheb_constants()
    constants = jnp.array(steps, F32)
    vmem = pl.BlockSpec(memory_space=pltpu.VMEM)
    smem = pl.BlockSpec(memory_space=pltpu.SMEM)
    hbm = pl.BlockSpec(memory_space=pl.ANY)
    dma = pltpu.SemaphoreType.DMA
    patches = (QN, PATCH)
    return pl.pallas_call(
        kernel,
        out_shape=(
            jax.ShapeDtypeStruct((1, BLK, COLS), F32),
            jax.ShapeDtypeStruct((1, QN * PATCH), F32),
        ),
        in_specs=[smem, hbm, hbm, vmem, smem, smem, vmem, smem, hbm, hbm],
        out_specs=(vmem, vmem),
        scratch_shapes=[
            pltpu.VMEM((1, BLK, COLS), BF16),
            pltpu.VMEM((1, BLK, BLK), F32),
            pltpu.VMEM((1, FAR, RANK, QN * PATCH), BF16),
            pltpu.VMEM((1, OWN, SUB * QN * PATCH), BF16),
            pltpu.VMEM((OWN, SUB * QN, PATCH), F32),
            pltpu.VMEM((BLK, 3 * BLK), BF16),
            pltpu.VMEM((BLK, VCOLS), F32),
            pltpu.VMEM((BLK, VCOLS), F32),
            pltpu.VMEM((BLK, VCOLS), F32),
            pltpu.VMEM(patches, F32),
            pltpu.VMEM((ZN,) + patches, F32),
            pltpu.VMEM((YN, 16, PATCH), jnp.int32),
            pltpu.VMEM((YN, NB * PATCH, PATCH), BF16),
            pltpu.VMEM((YN, FAR) + patches, F32),
            pltpu.VMEM((YN, FAR) + patches, F32),
            pltpu.VMEM((YN,) + patches, F32),
            pltpu.VMEM((YN,) + patches, F32),
            pltpu.VMEM((1, 256), F32),
            pltpu.VMEM((SUB, 1, 256), F32),
            pltpu.VMEM((2, 8) + patches, F32),
            pltpu.VMEM((2, 8) + patches, F32),
            pltpu.VMEM(patches, F32),
            pltpu.VMEM(patches, F32),
            pltpu.VMEM(patches, F32),
            pltpu.VMEM((BLK, 3 * PATCH), BF16),
            pltpu.VMEM((PATCH, 3 * PATCH), BF16),
            dma((4,)),
            dma((ZN,)),
            dma((ZN,)),
            dma((YN,)),
            dma((YN,)),
            dma((YN,)),
            dma((YN,)),
            dma((YN,)),
            dma((YN,)),
            dma((SUB,)),
            dma((SUB,)),
            dma((2, 8)),
            dma((2, 8)),
            dma((1,)),
            dma((1,)),
        ],
        name="robin_sweep",
        compiler_params=pltpu.CompilerParams(
            collective_id=0, has_side_effects=True, vmem_limit_bytes=40 * 1024 * 1024
        ),
    )(constants, *operands)


def solution(mesh):
    placed = (
        P("dom", None, "sub"),
        P("dom", None, None),
        P("dom", "sub"),
        P("dom", None),
        P("dom", None),
        P("dom", None, None),
        P("dom"),
        P("dom", None, None, "sub"),
        P("dom", "sub", None),
    )
    return jax.shard_map(
        body,
        mesh=mesh,
        in_specs=placed,
        out_specs=(P("dom", None, "sub"), P("dom", "sub")),
        check_vma=False,
    )
```

time: 931 us -> 91.1 us (0.10)
  blocking collectives: 507 us -> 0 us
  waiting for transfers between devices: 387 us -> 0 us
  Pallas kernels: 0 us -> 79.8 us
  between operations: 16.2 us -> 1.3 us
  matrix products: 13.7 us -> 0 us
    unnamed x2 -> x0, waiting for transfers between devices: 387 us -> none
    all_gather x1 -> x0, blocking collectives: 379 us -> none  [body(): gathered = lax.all_gather(traces_prev, 'dom', axis=0, tiled=True)]
    unnamed x1 -> x0, blocking collectives: 128 us -> none
    pallas_call x0 -> x1, Pallas kernels: none -> 79.8 us  [body(): pl.pallas_call(kernel, out_shape=(jax.ShapeDtypeStruct((1, BLK, COLS), F3...]
    dot_general x10 -> x0, matrix products: 13.7 us -> none  [the longest x7 10 us: apply_operator(): jnp.dot(stiff_block, vectors, precision=lax.Precision.HIGHEST, preferred_...]
  transfers between devices with their start and end apart: 1 -> 0, of which waited for: 1 -> 0; matrix products, arithmetic and copies ran while one was open for 0% -> 0% of each run, Pallas kernels for 0% -> 0%
where the time goes in v1:
time: 91.1 us; the launch traced here: 90.7 us
  Pallas kernels  79.8 us (88%)
  local copies, waits for them, and re-layouts  9.57 us (11%)
  between operations  1.3 us (1%)
    pallas_call x1, Pallas kernels, body(): pl.pallas_call(kernel, out_shape=(jax.ShapeDtypeStruct((1, BLK, COLS), F3...  79.8 us
    unnamed x20, local copies, waits for them, and re-layouts  9.57 us

profile of v1, /device:TPU:1, one launch (start us, length us, event | category | flops | bytes accessed | tf_op | source)
XLA Modules:
  0.0 90.7 jit_solution(9306869538428150685)
XLA Ops:
  1.3 0.0 copy-start
  1.3 1.4 %copy-done = bf16[1,2,192,2048]{3,2,1,0:T(8,128)(2,1)S(1)} copy-done((bf16[1,2,192,2048]{3,2,1,0:T(8,128)(2,1)S(1)}, bf16[1,2,192,2048]{3,2,1,0:T(8,128)(2,1)}, u32[]{:S(2)}) %copy-start) | copy-done | bytes 1572888
  2.7 0.0 copy-start.1
  2.7 1.2 %copy-done.1 = f32[1,512,512]{2,1,0:T(8,128)S(1)} copy-done((f32[1,512,512]{2,1,0:T(8,128)S(1)}, f32[1,512,512]{2,1,0:T(8,128)}, u32[]{:S(2)}) %copy-start.1) | copy-done | bytes 1048600
  3.9 0.0 copy-start.2
  3.9 1.2 %copy-done.2 = bf16[1,12,32768]{2,1,0:T(8,128)(2,1)S(1)} copy-done((bf16[1,12,32768]{2,1,0:T(8,128)(2,1)S(1)}, bf16[1,12,32768]{2,1,0:T(8,128)(2,1)}, u32[]{:S(2)}) %copy-start.2) | copy-done | bytes 786456
  5.1 0.0 copy-start.3
  5.1 0.9 %copy-done.3 = bf16[1,512,256]{2,1,0:T(8,128)(2,1)S(1)} copy-done((bf16[1,512,256]{2,1,0:T(8,128)(2,1)S(1)}, bf16[1,512,256]{2,1,0:T(8,128)(2,1)}, u32[]{:S(2)}) %copy-start.3) | copy-done | bytes 262168
  6.1 0.0 copy-start.4
  6.1 0.7 copy-done.4
  6.8 0.0 copy-start.5
  6.8 0.7 copy-done.5
  7.5 0.0 copy-start.6
  7.5 0.7 copy-done.6
  8.2 0.0 copy-start.7
  8.2 0.7 copy-done.7
  8.8 0.0 copy-start.8
  8.8 0.7 copy-done.8
  9.5 79.8 %robin_sweep.1 = (f32[1,512,256]{2,1,0:T(8,128)S(1)}, f32[1,2048]{1,0:T(1,128)S(1)}) custom-call(f32[7,2]{1,0:T(8,128)S(1)} %copy-done.5, bf16[1,512,256]{2,1,0:T(8,128)(2,1)S(1)} %copy-done.3, f32[1,512,512]{2,1,0:T(8,128)S(1)} %copy-done.1, f32[1,2048]{1,0:T(1,128)S(1)} %copy-done.4, s32[1,4]{1,0:T(1,128)S(1)} %copy-done.7, s32[1,2]{1,0:T(1,128)S(1)} %copy-done.8, ...), custom_call_target="tpu_custom_call" | custom-call | tf_op jit(solution)/shard_map/robin_sweep/pallas_call | solution.py:396
  89.3 0.8 copy.15
  90.1 0.6 copy.16
Async XLA Ops:
  1.3 1.4 %copy-start = (bf16[1,2,192,2048]{3,2,1,0:T(8,128)(2,1)S(1)}, bf16[1,2,192,2048]{3,2,1,0:T(8,128)(2,1)}, u32[]{:S(2)}) copy-start(bf16[1,2,192,2048]{3,2,1,0:T(8,128)(2,1)} %far_hbm.1) | copy-start | bytes 4718596
  2.7 1.2 %copy-start.1 = (f32[1,512,512]{2,1,0:T(8,128)S(1)}, f32[1,512,512]{2,1,0:T(8,128)}, u32[]{:S(2)}) copy-start(f32[1,512,512]{2,1,0:T(8,128)} %stiff_hbm.1) | copy-start | bytes 3145732
  3.9 1.2 %copy-start.2 = (bf16[1,12,32768]{2,1,0:T(8,128)(2,1)S(1)}, bf16[1,12,32768]{2,1,0:T(8,128)(2,1)}, u32[]{:S(2)}) copy-start(bf16[1,12,32768]{2,1,0:T(8,128)(2,1)} %basis_hbm.1) | copy-start | bytes 2359300
  5.1 0.9 %copy-start.3 = (bf16[1,512,256]{2,1,0:T(8,128)(2,1)S(1)}, bf16[1,512,256]{2,1,0:T(8,128)(2,1)}, u32[]{:S(2)}) copy-start(bf16[1,512,256]{2,1,0:T(8,128)(2,1)} %exc_hbm.1) | copy-start | bytes 786436
  6.1 0.7 copy-start.4
  6.8 0.7 copy-start.5
  7.5 0.7 copy-start.6
  8.2 0.7 copy-start.7
  8.8 0.7 copy-start.8

commit v2 on v1

--- a/solution.py
+++ b/solution.py
@@ -65,18 +65,22 @@
 
 
 def kernel(
-    coef_ref,
     exc_hbm,
     stiff_hbm,
+    trace_hbm,
+    neigh_hbm,
+    farl_hbm,
+    perm_hbm,
+    live_hbm,
+    far_hbm,
+    basis_hbm,
+    field_ref,
+    next_ref,
     trace_ref,
     neigh_ref,
     farl_ref,
     perm_ref,
     live_ref,
-    far_hbm,
-    basis_hbm,
-    field_ref,
-    next_ref,
     exc_v,
     stiff_v,
     far_v,
@@ -118,6 +122,8 @@
     pr,
     hs,
     hr,
+    side_sem,
+    ready_sem,
 ):
     dom = lax.axis_index("dom")
     sub = lax.axis_index("sub")
@@ -128,23 +134,35 @@
     def z_peer(k):
         return (((z + k) % ZN) * YN + y, sub)
 
+    def line_peer(at):
+        return (at * YN + y, sub)
+
     def y_peer(k):
         return (z * YN + (y + k) % YN, sub)
 
-    def s_peer(k):
-        return (dom, (sub + k) % SUB)
+    def s_peer(dx, dh, dc):
+        return (dom, ((x + dx) % XN) * 4 + ((h + dh) % 2) * 2 + (c + dc) % 2)
 
     def e_peer(k):
         t = (s8 + k) % 8
         return (dom, (t // 2) * 4 + h * 2 + t % 2)
 
     across = (dom, x * 4 + (1 - h) * 2 + c)
+    is_end = (z == 0) | (z == ZN - 1)
+    touching = ((ZN - 1 - z) * YN + y, x * 4 + (1 - h) * 2 + c)
+
+    def signal(sem, peer):
+        pl.semaphore_signal(sem, inc=1, device_id=peer, device_id_type=MESH)
 
     barrier = pltpu.get_barrier_semaphore()
     peers = [z_peer(k) for k in range(1, ZN)] + [y_peer(k) for k in range(1, YN)]
-    peers += [s_peer(k) for k in range(1, SUB)]
+    peers += [e_peer(k) for k in range(1, 8)]
     for peer in peers:
-        pl.semaphore_signal(barrier, inc=1, device_id=peer, device_id_type=MESH)
+        signal(barrier, peer)
+
+    @pl.when(is_end)
+    def _():
+        signal(barrier, touching)
 
     loads = [
         pltpu.make_async_copy(stiff_hbm, stiff_v, lsem.at[0]),
@@ -152,8 +170,19 @@
         pltpu.make_async_copy(basis_hbm, basis_v, lsem.at[2]),
         pltpu.make_async_copy(far_hbm, far_v, lsem.at[3]),
     ]
+    smalls = [
+        pltpu.make_async_copy(trace_hbm, trace_ref, lsem.at[4]),
+        pltpu.make_async_copy(perm_hbm, perm_ref, lsem.at[5]),
+        pltpu.make_async_copy(neigh_hbm, neigh_ref, lsem.at[6]),
+        pltpu.make_async_copy(farl_hbm, farl_ref, lsem.at[7]),
+        pltpu.make_async_copy(live_hbm, live_ref, lsem.at[8]),
+    ]
+    for load in smalls:
+        load.start()
     for load in loads:
         load.start()
+    for load in smalls:
+        load.wait()
 
     for q in range(QN):
         own_t[q : q + 1, :] = trace_ref[:, q * PATCH : (q + 1) * PATCH]
@@ -164,43 +193,8 @@
     for f in range(FAR):
         tab_v[0, 8 + f : 9 + f, :] = jnp.full((1, PATCH), farl_ref[0, f], jnp.int32)
     tab_v[0, 10:16, :] = jnp.zeros((6, PATCH), jnp.int32)
-
-    loads[0].wait()
-    row = iota((BLK, BLK), 0)
-    col = iota((BLK, BLK), 1)
-    operator = stiff_v[0] + jnp.where((row == col) & (row < TROW), robin_gain, 0.0)
-    a_high, a_low = split2(operator)
-    a3[:, 0:BLK] = a_high
-    a3[:, BLK : 2 * BLK] = a_low
-    a3[:, 2 * BLK : 3 * BLK] = a_high
-
     live = live_ref[0]
-    loads[1].wait()
-    column = sub * COLS + iota((BLK, COLS), 1)
-    r_v[:, 0:COLS] = jnp.where(column < live, exc_v[0].astype(F32), 0.0)
-    r_v[:, COLS:] = jnp.where(iota((BLK, PATCH), 0) == iota((BLK, PATCH), 1) % TROW, 1.0, 0.0)
-    centre, _ = cheb_constants()
-    first = r_v[...] * (1.0 / centre)
-    u_v[...] = first
-    x_v[...] = first
-
-    def smooth(step, carry):
-        u_high, u_low = split2(u_v[...])
-        moved = jnp.dot(
-            a3[...],
-            jnp.concatenate([u_high, u_high, u_low], axis=0),
-            preferred_element_type=F32,
-        )
-        res = r_v[...] - moved
-        r_v[...] = res
-        following = coef_ref[step, 0] * u_v[...] + coef_ref[step, 1] * res
-        u_v[...] = following
-        x_v[...] += following
-        return carry
-
-    lax.fori_loop(0, 4, smooth, 0)
-
-    pl.semaphore_wait(barrier, len(peers))
+    centre, steps = cheb_constants()
 
     def remote(src, dst, send, recv, peer):
         return pltpu.make_async_remote_copy(
@@ -213,45 +207,121 @@
         )
 
     z_copies = [
-        remote(own_t, rows_v.at[z], zs.at[k], zr.at[k], z_peer(k)) for k in range(1, ZN)
+        remote(own_t, rows_v.at[z], zs.at[k], zr.at[k], z_peer(k))
+        for k in (8, 7, 9, 6, 10, 5, 11, 4, 12, 3, 13, 2, 14, 1, 15)
     ]
     t_copies = [
         remote(tab_v.at[0], tab_v.at[YN - k], ts.at[k], tr.at[k], y_peer(k)) for k in range(1, YN)
     ]
-    for copy in z_copies:
-        copy.start()
-    for copy in t_copies:
-        copy.start()
-
-    lax.fori_loop(4, DEG - 1, smooth, 0)
-
-    loads[2].wait()
-    for r in range(OWN):
-        basis_d[r] = basis_v[0, r : r + 1, :].astype(F32).reshape(256, PATCH)
+
+    def meet_and_send():
+        pl.semaphore_wait(barrier, len(peers) + is_end.astype(jnp.int32))
+        for copy in z_copies:
+            copy.start()
+        for copy in t_copies:
+            copy.start()
+
+        @pl.when(is_end)
+        def _():
+            for k in range(1, 8):
+                signal(side_sem, e_peer(k))
+            pl.semaphore_wait(side_sem, 7)
+            signal(ready_sem, touching)
+
+    early = (h == 0) & (z < ZN // 2)
+
+    def pass_on(chosen):
+        @pl.when(is_end & chosen)
+        def _():
+            pl.semaphore_wait(ready_sem, 1)
+            for k in range(1, 8):
+                signal(ready_sem, line_peer(jnp.where(z == 0, k, ZN - 1 - k)))
+
+    def local_work():
+        smooth_part()
+        pass_on(jnp.logical_not(early))
+        prepare_part()
+
+    def smooth_part():
+        loads[0].wait()
+        row = iota((BLK, BLK), 0)
+        col = iota((BLK, BLK), 1)
+        operator = stiff_v[0] + jnp.where((row == col) & (row < TROW), robin_gain, 0.0)
+        a_high, a_low = split2(operator)
+        a3[:, 0:BLK] = a_high
+        a3[:, BLK : 2 * BLK] = a_low
+        a3[:, 2 * BLK : 3 * BLK] = a_high
+
+        loads[1].wait()
+        column = sub * COLS + iota((BLK, COLS), 1)
+        r_v[:, 0:COLS] = jnp.where(column < live, exc_v[0].astype(F32), 0.0)
+        r_v[:, COLS:] = jnp.where(iota((BLK, PATCH), 0) == iota((BLK, PATCH), 1) % TROW, 1.0, 0.0)
+        first = r_v[...] * (1.0 / centre)
+        u_v[...] = first
+        x_v[...] = first
+
+        def smooth(step, carry):
+            u_high, u_low = split2(u_v[...])
+            moved = jnp.dot(
+                a3[...],
+                jnp.concatenate([u_high, u_high, u_low], axis=0),
+                preferred_element_type=F32,
+            )
+            res = r_v[...] - moved
+            r_v[...] = res
+            keep, add = steps[0]
+            for at in range(1, DEG - 1):
+                keep = jnp.where(step == at, steps[at][0], keep)
+                add = jnp.where(step == at, steps[at][1], add)
+            following = keep * u_v[...] + add * res
+            u_v[...] = following
+            x_v[...] += following
+            return carry
+
+        lax.fori_loop(0, DEG - 1, smooth, 0)
 
     lane = iota((PATCH, PATCH), 1)
     sublane = iota((PATCH, PATCH), 0)
-    g_high, g_low = split2(x_v[:, COLS:])
-    g3_v[:, 0:PATCH] = g_high
-    g3_v[:, PATCH : 2 * PATCH] = g_high
-    g3_v[:, 2 * PATCH :] = g_low
-    tiled = jnp.concatenate([x_v[0:TROW, COLS:]] * QN, axis=0)
-    gain = jnp.where(lane // TROW == sublane // TROW, (2.0 * robin_gain) * tiled, 0.0)
-    b_high, b_low = split2(gain)
-    b3_v[:, 0:PATCH] = b_high
-    b3_v[:, PATCH : 2 * PATCH] = b_high
-    b3_v[:, 2 * PATCH :] = b_low
-
-    pieces = split3((2.0 * robin_gain) * x_v[0:TROW, 0:COLS])
-    stacked = jnp.concatenate([piece.astype(F32) for piece in pieces], axis=0).astype(BF16)
-    spread = iota((COLS, PATCH), 1) // TROW
-    place = iota((COLS, PATCH), 0)
-    keep = iota((TROW, PATCH), 0) == iota((TROW, PATCH), 1) % TROW
-    for q in range(QN):
-        pick = jnp.where(place == q * 16 + spread, 1.0, 0.0).astype(BF16)
-        got = jnp.dot(stacked, pick, preferred_element_type=F32)
-        got = got[0:8] + got[8:16] + got[16:24]
-        t0_v[q : q + 1, :] = jnp.sum(jnp.where(keep, got, 0.0), axis=0, keepdims=True)
+
+    def prepare_part():
+        loads[2].wait()
+        for r in range(OWN):
+            basis_d[r] = basis_v[0, r : r + 1, :].astype(F32).reshape(256, PATCH)
+
+        g_high, g_low = split2(x_v[:, COLS:])
+        g3_v[:, 0:PATCH] = g_high
+        g3_v[:, PATCH : 2 * PATCH] = g_high
+        g3_v[:, 2 * PATCH :] = g_low
+        tiled = jnp.concatenate([x_v[0:TROW, COLS:]] * QN, axis=0)
+        gain = jnp.where(lane // TROW == sublane // TROW, (2.0 * robin_gain) * tiled, 0.0)
+        b_high, b_low = split2(gain)
+        b3_v[:, 0:PATCH] = b_high
+        b3_v[:, PATCH : 2 * PATCH] = b_high
+        b3_v[:, 2 * PATCH :] = b_low
+
+        pieces = split3((2.0 * robin_gain) * x_v[0:TROW, 0:COLS])
+        stacked = jnp.concatenate([piece.astype(F32) for piece in pieces], axis=0).astype(BF16)
+        spread = iota((COLS, PATCH), 1) // TROW
+        place = iota((COLS, PATCH), 0)
+        keep = iota((TROW, PATCH), 0) == iota((TROW, PATCH), 1) % TROW
+        for q in range(QN):
+            pick = jnp.where(place == q * 16 + spread, 1.0, 0.0).astype(BF16)
+            got = jnp.dot(stacked, pick, preferred_element_type=F32)
+            got = got[0:8] + got[8:16] + got[16:24]
+            t0_v[q : q + 1, :] = jnp.sum(jnp.where(keep, got, 0.0), axis=0, keepdims=True)
+
+    def phase(at, carry):
+        @pl.when((at == 0) != early)
+        def _():
+            meet_and_send()
+
+        @pl.when(at == 0)
+        def _():
+            local_work()
+
+        return carry
+
+    lax.fori_loop(0, 2, phase, 0)
 
     for copy in t_copies:
         copy.wait_recv()
@@ -279,6 +349,7 @@
             copy = remote(fsend.at[t], frecv.at[t], fs.at[t], fr.at[t], y_peer(t))
             copy.start()
             f_copies.append(copy)
+    pass_on(early)
     n_copies = []
     for t in (2, 1, 3, 0):
         faces = jnp.concatenate([pick_row(t, 4 + j) for j in range(NB)], axis=1)
@@ -303,11 +374,20 @@
     csend[:, 0:RANK] = partial[0:1, :]
     csend[:, RANK:] = jnp.zeros((1, 256 - RANK), F32)
     crecv[0] = csend[...]
-    c_copies = [
-        remote(csend, crecv.at[k], cs.at[k], cr.at[k], s_peer(k)) for k in range(1, SUB)
-    ]
-    for copy in c_copies:
-        copy.start()
+
+    @pl.when(jnp.logical_not(is_end))
+    def _():
+        pl.semaphore_wait(ready_sem, 1)
+
+    c_copies = []
+    for dh in (1, 0):
+        for dx in (2, 1, 3, 0):
+            for dc in (0, 1):
+                at = dh * 8 + dx * 2 + dc
+                if at:
+                    copy = remote(csend, crecv.at[at], cs.at[at], cr.at[at], s_peer(dx, dh, dc))
+                    copy.start()
+                    c_copies.append(copy)
     for copy in c_copies:
         copy.wait_recv()
 
@@ -386,11 +466,8 @@
 
 
 def body(*operands):
-    _, steps = cheb_constants()
-    constants = jnp.array(steps, F32)
     vmem = pl.BlockSpec(memory_space=pltpu.VMEM)
-    smem = pl.BlockSpec(memory_space=pltpu.SMEM)
-    hbm = pl.BlockSpec(memory_space=pl.ANY)
+    hbm = pl.BlockSpec(memory_space=pltpu.HBM)
     dma = pltpu.SemaphoreType.DMA
     patches = (QN, PATCH)
     return pl.pallas_call(
@@ -399,9 +476,14 @@
             jax.ShapeDtypeStruct((1, BLK, COLS), F32),
             jax.ShapeDtypeStruct((1, QN * PATCH), F32),
         ),
-        in_specs=[smem, hbm, hbm, vmem, smem, smem, vmem, smem, hbm, hbm],
+        in_specs=[hbm] * 9,
         out_specs=(vmem, vmem),
         scratch_shapes=[
+            pltpu.VMEM((1, QN * PATCH), F32),
+            pltpu.SMEM((1, NB), jnp.int32),
+            pltpu.SMEM((1, FAR), jnp.int32),
+            pltpu.VMEM((1, NB, PATCH), jnp.int32),
+            pltpu.SMEM((1,), jnp.int32),
             pltpu.VMEM((1, BLK, COLS), BF16),
             pltpu.VMEM((1, BLK, BLK), F32),
             pltpu.VMEM((1, FAR, RANK, QN * PATCH), BF16),
@@ -428,7 +510,7 @@
             pltpu.VMEM(patches, F32),
             pltpu.VMEM((BLK, 3 * PATCH), BF16),
             pltpu.VMEM((PATCH, 3 * PATCH), BF16),
-            dma((4,)),
+            dma((9,)),
             dma((ZN,)),
             dma((ZN,)),
             dma((YN,)),
@@ -443,12 +525,14 @@
             dma((2, 8)),
             dma((1,)),
             dma((1,)),
+            pltpu.SemaphoreType.REGULAR,
+            pltpu.SemaphoreType.REGULAR,
         ],
         name="robin_sweep",
         compiler_params=pltpu.CompilerParams(
-            collective_id=0, has_side_effects=True, vmem_limit_bytes=40 * 1024 * 1024
+            collective_id=0, has_side_effects=True, vmem_limit_bytes=60 * 1024 * 1024
         ),
-    )(constants, *operands)
+    )(*operands)
 
 
 def solution(mesh):

time: 91.1 us -> 78.7 us (0.86)
  local copies, waits for them, and re-layouts: 9.57 us -> 3.16 us
  Pallas kernels: 79.8 us -> 74 us
    unnamed x20 -> x2, local copies, waits for them, and re-layouts: 9.57 us -> 3.16 us
    pallas_call x1, Pallas kernels: 79.8 us -> 74 us  [body(): pl.pallas_call(kernel, out_shape=(jax.ShapeDtypeStruct((1, BLK, COLS), F3...]
where the time goes in v2:
time: 78.7 us; the launch traced here: 78.4 us
  Pallas kernels  74 us (94%)
  local copies, waits for them, and re-layouts  3.16 us (4%)
  between operations  1.29 us (2%)
    pallas_call x1, Pallas kernels, body(): pl.pallas_call(kernel, out_shape=(jax.ShapeDtypeStruct((1, BLK, COLS), F3...  74 us
    unnamed x2, local copies, waits for them, and re-layouts  3.16 us

profile of v2, /device:TPU:1, one launch (start us, length us, event | category | flops | bytes accessed | tf_op | source)
XLA Modules:
  0.0 78.4 jit_solution(14878584180074912554)
XLA Ops:
  1.3 74.0 %robin_sweep.1 = (f32[1,512,256]{2,1,0:T(8,128)}, f32[1,2048]{1,0:T(1,128)}) custom-call(bf16[1,512,256]{2,1,0:T(8,128)(2,1)} %exc_hbm.1, f32[1,512,512]{2,1,0:T(8,128)} %stiff_hbm.1, f32[1,2048]{1,0:T(1,128)} %trace_hbm.1, s32[1,4]{1,0:T(1,128)} %neigh_hbm.1, s32[1,2]{1,0:T(1,128)} %farl_hbm.1, s32[1,4,128]{2,1,0:T(4,128)} %perm_hbm.1, ...), custom_call_target="tpu_custom_call" | custom-call | tf_op jit(solution)/shard_map/robin_sweep/pallas_call | solution.py:473
  75.3 1.9 %copy.14 = f32[1,512,256]{2,1,0:T(8,128)} copy(f32[1,512,256]{2,1,0:T(8,128)} %get-tuple-element.4) | data formatting | bytes 1048576
  77.1 1.3 %copy.15 = f32[1,2048]{1,0:T(1,128)} copy(f32[1,2048]{1,0:T(1,128)} %get-tuple-element.5) | data formatting | bytes 16384

commit v3 on v2

--- a/solution.py
+++ b/solution.py
@@ -90,8 +90,10 @@
     u_v,
     r_v,
     x_v,
-    own_t,
-    rows_v,
+    own_hi,
+    own_lo,
+    rows_hi,
+    rows_lo,
     tab_v,
     sel_v,
     fsend,
@@ -124,6 +126,8 @@
     hr,
     side_sem,
     ready_sem,
+    hub_sem,
+    up_sem,
 ):
     dom = lax.axis_index("dom")
     sub = lax.axis_index("sub")
@@ -148,28 +152,21 @@
         return (dom, (t // 2) * 4 + h * 2 + t % 2)
 
     across = (dom, x * 4 + (1 - h) * 2 + c)
+    first, second = h == 0, h == 1
     is_end = (z == 0) | (z == ZN - 1)
     touching = ((ZN - 1 - z) * YN + y, x * 4 + (1 - h) * 2 + c)
+    direct = second | (z < ZN // 2)
+    hub = first & (z == ZN // 2 - 1)
+
+    turned = jnp.where(z < ZN // 2, ZN - 1 - z, z)
+
+    def line_at(i):
+        place = i + (i >= turned).astype(jnp.int32)
+        return jnp.where(z < ZN // 2, ZN - 1 - place, place)
 
     def signal(sem, peer):
         pl.semaphore_signal(sem, inc=1, device_id=peer, device_id_type=MESH)
 
-    barrier = pltpu.get_barrier_semaphore()
-    peers = [z_peer(k) for k in range(1, ZN)] + [y_peer(k) for k in range(1, YN)]
-    peers += [e_peer(k) for k in range(1, 8)]
-    for peer in peers:
-        signal(barrier, peer)
-
-    @pl.when(is_end)
-    def _():
-        signal(barrier, touching)
-
-    loads = [
-        pltpu.make_async_copy(stiff_hbm, stiff_v, lsem.at[0]),
-        pltpu.make_async_copy(exc_hbm, exc_v, lsem.at[1]),
-        pltpu.make_async_copy(basis_hbm, basis_v, lsem.at[2]),
-        pltpu.make_async_copy(far_hbm, far_v, lsem.at[3]),
-    ]
     smalls = [
         pltpu.make_async_copy(trace_hbm, trace_ref, lsem.at[4]),
         pltpu.make_async_copy(perm_hbm, perm_ref, lsem.at[5]),
@@ -179,14 +176,42 @@
     ]
     for load in smalls:
         load.start()
+
+    barrier = pltpu.get_barrier_semaphore()
+    side_peers = [y_peer(k) for k in range(1, YN)] + [e_peer(k) for k in range(1, 8)]
+    for i in range(ZN - 1):
+        at = line_at(i)
+
+        @pl.when(second | (at > z))
+        def _():
+            signal(barrier, line_peer(at))
+
+    @pl.when(direct)
+    def _():
+        for peer in side_peers:
+            signal(barrier, peer)
+
+    @pl.when(first & is_end)
+    def _():
+        signal(barrier, touching)
+
+    loads = [
+        pltpu.make_async_copy(stiff_hbm, stiff_v, lsem.at[0]),
+        pltpu.make_async_copy(exc_hbm, exc_v, lsem.at[1]),
+        pltpu.make_async_copy(basis_hbm, basis_v, lsem.at[2]),
+        pltpu.make_async_copy(far_hbm, far_v, lsem.at[3]),
+    ]
     for load in loads:
         load.start()
     for load in smalls:
         load.wait()
 
-    for q in range(QN):
-        own_t[q : q + 1, :] = trace_ref[:, q * PATCH : (q + 1) * PATCH]
-    rows_v[z] = own_t[...]
+    own = jnp.concatenate([trace_ref[:, q * PATCH : (q + 1) * PATCH] for q in range(QN)], axis=0)
+    high, low = split2(own)
+    own_hi[...] = high
+    own_lo[...] = low
+    rows_hi[z] = high
+    rows_lo[z] = low
     tab_v[0, 0:4, :] = perm_ref[0]
     for j in range(NB):
         tab_v[0, 4 + j : 5 + j, :] = jnp.full((1, PATCH), neigh_ref[0, j], jnp.int32)
@@ -206,40 +231,91 @@
             device_id_type=MESH,
         )
 
-    z_copies = [
-        remote(own_t, rows_v.at[z], zs.at[k], zr.at[k], z_peer(k))
-        for k in (8, 7, 9, 6, 10, 5, 11, 4, 12, 3, 13, 2, 14, 1, 15)
-    ]
+    def z_start(own_ref, rows_ref, part, chosen):
+        for i in range(ZN - 1):
+            at = line_at(i)
+
+            @pl.when(chosen(at))
+            def _():
+                remote(
+                    own_ref, rows_ref.at[z], zs.at[part, at], zr.at[part, z], line_peer(at)
+                ).start()
+
+    def z_wait(own_ref, rows_ref, part):
+        for i in range(ZN - 1):
+            at = line_at(i)
+            remote(own_ref, rows_ref.at[at], zs.at[part, at], zr.at[part, at], line_peer(at)).wait_recv()
+
+    def z_sent(own_ref, rows_ref, part):
+        for i in range(ZN - 1):
+            at = line_at(i)
+            remote(own_ref, rows_ref.at[z], zs.at[part, at], zr.at[part, z], line_peer(at)).wait_send()
+
     t_copies = [
         remote(tab_v.at[0], tab_v.at[YN - k], ts.at[k], tr.at[k], y_peer(k)) for k in range(1, YN)
     ]
 
     def meet_and_send():
-        pl.semaphore_wait(barrier, len(peers) + is_end.astype(jnp.int32))
-        for copy in z_copies:
-            copy.start()
-        for copy in t_copies:
-            copy.start()
-
-        @pl.when(is_end)
+        expected = jnp.where(second, ZN - 1, z) + len(side_peers) * direct.astype(jnp.int32)
+        pl.semaphore_wait(barrier, expected + (second & is_end).astype(jnp.int32))
+
+        @pl.when(second & is_end)
         def _():
             for k in range(1, 8):
                 signal(side_sem, e_peer(k))
+
+        z_start(own_hi, rows_hi, 0, lambda at: second | (at < z))
+        for i in range(ZN - 1):
+            at = line_at(i)
+
+            @pl.when(first & (at < z))
+            def _():
+                signal(up_sem, line_peer(at))
+
+        @pl.when(direct)
+        def _():
+            for copy in t_copies:
+                copy.start()
+
+        @pl.when(second & is_end)
+        def _():
             pl.semaphore_wait(side_sem, 7)
             signal(ready_sem, touching)
 
-    early = (h == 0) & (z < ZN // 2)
-
-    def pass_on(chosen):
-        @pl.when(is_end & chosen)
-        def _():
-            pl.semaphore_wait(ready_sem, 1)
+    def answer_line():
+        @pl.when(z < ZN - 1)
+        def _():
+            pl.semaphore_wait(up_sem, ZN - 1 - z)
+
+        @pl.when(z == 0)
+        def _():
             for k in range(1, 8):
-                signal(ready_sem, line_peer(jnp.where(z == 0, k, ZN - 1 - k)))
+                signal(side_sem, e_peer(k))
+
+        @pl.when(hub)
+        def _():
+            for peer in side_peers:
+                signal(side_sem, peer)
+
+        z_start(own_hi, rows_hi, 0, lambda at: at > z)
+
+        @pl.when(hub)
+        def _():
+            pl.semaphore_wait(side_sem, len(side_peers))
+            for at in range(ZN // 2, ZN):
+                signal(hub_sem, line_peer(at))
+
+    def pass_on():
+        for k in range(1, 8):
+            signal(ready_sem, line_peer(jnp.where(z == 0, k, ZN - 1 - k)))
+
+    def return_word():
+        pl.semaphore_wait(ready_sem, 1)
+        signal(ready_sem, touching)
+        pass_on()
 
     def local_work():
         smooth_part()
-        pass_on(jnp.logical_not(early))
         prepare_part()
 
     def smooth_part():
@@ -311,7 +387,7 @@
             t0_v[q : q + 1, :] = jnp.sum(jnp.where(keep, got, 0.0), axis=0, keepdims=True)
 
     def phase(at, carry):
-        @pl.when((at == 0) != early)
+        @pl.when((at == 0) == first)
         def _():
             meet_and_send()
 
@@ -322,6 +398,25 @@
         return carry
 
     lax.fori_loop(0, 2, phase, 0)
+
+    @pl.when(first)
+    def _():
+        answer_line()
+
+    @pl.when(jnp.logical_not(direct))
+    def _():
+        pl.semaphore_wait(hub_sem, 1)
+        for copy in t_copies:
+            copy.start()
+
+    @pl.when(first & (z == ZN - 1))
+    def _():
+        return_word()
+
+    @pl.when(second & is_end)
+    def _():
+        pl.semaphore_wait(ready_sem, 1)
+        pass_on()
 
     for copy in t_copies:
         copy.wait_recv()
@@ -331,43 +426,39 @@
             sel_v[t, j * PATCH : (j + 1) * PATCH, :] = jnp.where(hit, 1.0, 0.0).astype(BF16)
 
     loads[3].wait()
-    for copy in z_copies:
-        copy.wait_recv()
-
-    def pick_row(t, entry):
+    z_wait(own_hi, rows_hi, 0)
+
+    def pick_row(t, entry, rows):
         wanted = jnp.broadcast_to(tab_v[t, entry : entry + 1, :], (QN, PATCH))
         found = jnp.zeros((QN, PATCH), F32)
         for k in range(ZN):
-            found = jnp.where(wanted == k * YN + y, rows_v[k], found)
+            found = jnp.where(wanted == k * YN + y, rows[k], found)
         return found
 
     f_copies = []
+    high_rows = [rows_hi[k].astype(F32) for k in range(ZN)]
     for t in (2, 1, 3, 0):
         for f in range(FAR):
-            fsend[t, f] = pick_row(t, 8 + f)
+            fsend[t, f] = pick_row(t, 8 + f, high_rows).astype(BF16)
         if t:
             copy = remote(fsend.at[t], frecv.at[t], fs.at[t], fr.at[t], y_peer(t))
             copy.start()
             f_copies.append(copy)
-    pass_on(early)
-    n_copies = []
-    for t in (2, 1, 3, 0):
-        faces = jnp.concatenate([pick_row(t, 4 + j) for j in range(NB)], axis=1)
-        three = split3(faces)
-        got = jnp.dot(
-            jnp.concatenate(three, axis=0), sel_v[t], preferred_element_type=F32
-        )
-        nsend[t] = (got[0:QN] + got[QN : 2 * QN]) + got[2 * QN :]
-        if t:
-            copy = remote(nsend.at[t], nrecv.at[t], ns.at[t], nr.at[t], y_peer(t))
-            copy.start()
-            n_copies.append(copy)
+    z_start(own_lo, rows_lo, 1, lambda at: at >= 0)
+
+    @pl.when(first & (z == 0))
+    def _():
+        pl.semaphore_wait(side_sem, 7)
+        return_word()
+
 
     for copy in f_copies:
         copy.wait_recv()
     partial = jnp.zeros((8, RANK), F32)
     for f in range(FAR):
-        remote_rows = ((fsend[0, f] + frecv[1, f]) + (frecv[2, f] + frecv[3, f])).astype(BF16).astype(F32)
+        remote_rows = fsend[0, f].astype(F32)
+        for t in range(1, YN):
+            remote_rows += frecv[t, f].astype(F32)
         flat = jnp.concatenate([remote_rows[q : q + 1, :] for q in range(QN)], axis=1)
         flat = jnp.broadcast_to(flat, (8, QN * PATCH)).astype(BF16)
         partial += dot_nt(flat, far_v[0, f])
@@ -428,6 +519,20 @@
     h_copy = remote(hsend, hrecv, hs.at[0], hr.at[0], across)
     h_copy.start()
 
+    z_wait(own_lo, rows_lo, 1)
+    full_rows = [rows_hi[k].astype(F32) + rows_lo[k].astype(F32) for k in range(ZN)]
+    n_copies = []
+    for t in (2, 1, 3, 0):
+        faces = jnp.concatenate([pick_row(t, 4 + j, full_rows) for j in range(NB)], axis=1)
+        got = jnp.dot(
+            jnp.concatenate(split2(faces), axis=0), sel_v[t], preferred_element_type=F32
+        )
+        nsend[t] = got[0:QN] + got[QN:]
+        if t:
+            copy = remote(nsend.at[t], nrecv.at[t], ns.at[t], nr.at[t], y_peer(t))
+            copy.start()
+            n_copies.append(copy)
+
     for copy in n_copies:
         copy.wait_recv()
     near = (nsend[0] + nrecv[1]) + (nrecv[2] + nrecv[3])
@@ -460,7 +565,9 @@
     ).astype(BF16)
     field_ref[0] = x_v[:, 0:COLS] + dot_nt(g3_v[...], wide)
 
-    for copy in z_copies + t_copies + f_copies + n_copies + c_copies + p_copies[0] + p_copies[1]:
+    z_sent(own_hi, rows_hi, 0)
+    z_sent(own_lo, rows_lo, 1)
+    for copy in t_copies + f_copies + n_copies + c_copies + p_copies[0] + p_copies[1]:
         copy.wait_send()
     h_copy.wait_send()
 
@@ -493,12 +600,14 @@
             pltpu.VMEM((BLK, VCOLS), F32),
             pltpu.VMEM((BLK, VCOLS), F32),
             pltpu.VMEM((BLK, VCOLS), F32),
-            pltpu.VMEM(patches, F32),
-            pltpu.VMEM((ZN,) + patches, F32),
+            pltpu.VMEM(patches, BF16),
+            pltpu.VMEM(patches, BF16),
+            pltpu.VMEM((ZN,) + patches, BF16),
+            pltpu.VMEM((ZN,) + patches, BF16),
             pltpu.VMEM((YN, 16, PATCH), jnp.int32),
             pltpu.VMEM((YN, NB * PATCH, PATCH), BF16),
-            pltpu.VMEM((YN, FAR) + patches, F32),
-            pltpu.VMEM((YN, FAR) + patches, F32),
+            pltpu.VMEM((YN, FAR) + patches, BF16),
+            pltpu.VMEM((YN, FAR) + patches, BF16),
             pltpu.VMEM((YN,) + patches, F32),
             pltpu.VMEM((YN,) + patches, F32),
             pltpu.VMEM((1, 256), F32),
@@ -511,8 +620,8 @@
             pltpu.VMEM((BLK, 3 * PATCH), BF16),
             pltpu.VMEM((PATCH, 3 * PATCH), BF16),
             dma((9,)),
-            dma((ZN,)),
-            dma((ZN,)),
+            dma((2, ZN)),
+            dma((2, ZN)),
             dma((YN,)),
             dma((YN,)),
             dma((YN,)),
@@ -527,12 +636,14 @@
             dma((1,)),
             pltpu.SemaphoreType.REGULAR,
             pltpu.SemaphoreType.REGULAR,
+            pltpu.SemaphoreType.REGULAR,
+            pltpu.SemaphoreType.REGULAR,
         ],
         name="robin_sweep",
         compiler_params=pltpu.CompilerParams(
-            collective_id=0, has_side_effects=True, vmem_limit_bytes=60 * 1024 * 1024
+            collective_id=0, has_side_effects=True, vmem_limit_bytes=40 * 1024 * 1024
         ),
-    )(*operands)
+    )(*[o if o.ndim == 1 else pltpu.with_memory_space_constraint(o, pltpu.HBM) for o in operands])
 
 
 def solution(mesh):

time: 78.7 us -> 70.7 us (0.90)
  Pallas kernels: 74 us -> 67.8 us
  local copies, waits for them, and re-layouts: 3.16 us -> 1.39 us
    pallas_call x1, Pallas kernels: 74 us -> 67.8 us  [body(): pl.pallas_call(kernel, out_shape=(jax.ShapeDtypeStruct((1, BLK, COLS), F3...]
    unnamed x2, local copies, waits for them, and re-layouts: 3.16 us -> 1.39 us
where the time goes in v3:
time: 70.7 us; the launch traced here: 70.5 us
  Pallas kernels  67.8 us (96%)
  local copies, waits for them, and re-layouts  1.39 us (2%)
  between operations  1.29 us (2%)
    pallas_call x1, Pallas kernels, body(): pl.pallas_call(kernel, out_shape=(jax.ShapeDtypeStruct((1, BLK, COLS), F3...  67.8 us

profile of v3, /device:TPU:1, one launch (start us, length us, event | category | flops | bytes accessed | tf_op | source)
XLA Modules:
  0.0 70.5 jit_solution(6231815536764503429)
XLA Ops:
  1.3 67.8 %robin_sweep.1 = (f32[1,512,256]{2,1,0:T(8,128)S(1)}, f32[1,2048]{1,0:T(1,128)S(1)}) custom-call(bf16[1,512,256]{2,1,0:T(8,128)(2,1)} %exc_hbm.1, f32[1,512,512]{2,1,0:T(8,128)} %stiff_hbm.1, f32[1,2048]{1,0:T(1,128)} %trace_hbm.1, s32[1,4]{1,0:T(1,128)} %neigh_hbm.1, s32[1,2]{1,0:T(1,128)} %farl_hbm.1, s32[1,4,128]{2,1,0:T(4,128)} %perm_hbm.1, ...), custom_call_target="tpu_custom_call" | custom-call | tf_op jit(solution)/shard_map/robin_sweep/pallas_call | solution.py:580
  69.1 0.8 %copy.14 = f32[1,512,256]{2,1,0:T(8,128)} copy(f32[1,512,256]{2,1,0:T(8,128)S(1)} %get-tuple-element.4) | data formatting | bytes 1048576
  69.9 0.6 copy.15

commit v4 on v3

--- a/solution.py
+++ b/solution.py
@@ -104,8 +104,8 @@
     crecv,
     psend,
     precv,
-    hsend,
-    hrecv,
+    psend_b,
+    precv_b,
     t0_v,
     g3_v,
     b3_v,
@@ -151,12 +151,16 @@
         t = (s8 + k) % 8
         return (dom, (t // 2) * 4 + h * 2 + t % 2)
 
-    across = (dom, x * 4 + (1 - h) * 2 + c)
     first, second = h == 0, h == 1
     is_end = (z == 0) | (z == ZN - 1)
     touching = ((ZN - 1 - z) * YN + y, x * 4 + (1 - h) * 2 + c)
     direct = second | (z < ZN // 2)
     hub = first & (z == ZN // 2 - 1)
+
+    special = first & (y == 0) & (x == 0) & (c == 0)
+    beyond = special & (z >= ZN // 2)
+    origin = special & (z == 0)
+    relay = special & (z == 1)
 
     turned = jnp.where(z < ZN // 2, ZN - 1 - z, z)
 
@@ -182,7 +186,7 @@
     for i in range(ZN - 1):
         at = line_at(i)
 
-        @pl.when(second | (at > z))
+        @pl.when(second | ((at > z) & jnp.logical_not(origin & (at >= ZN // 2))))
         def _():
             signal(barrier, line_peer(at))
 
@@ -241,22 +245,38 @@
                     own_ref, rows_ref.at[z], zs.at[part, at], zr.at[part, z], line_peer(at)
                 ).start()
 
-    def z_wait(own_ref, rows_ref, part):
+    def z_wait(own_ref, rows_ref, part, chosen):
         for i in range(ZN - 1):
             at = line_at(i)
-            remote(own_ref, rows_ref.at[at], zs.at[part, at], zr.at[part, at], line_peer(at)).wait_recv()
-
-    def z_sent(own_ref, rows_ref, part):
+
+            @pl.when(chosen(at))
+            def _():
+                remote(
+                    own_ref, rows_ref.at[at], zs.at[part, at], zr.at[part, at], line_peer(at)
+                ).wait_recv()
+
+    def z_sent(own_ref, rows_ref, part, chosen):
         for i in range(ZN - 1):
             at = line_at(i)
-            remote(own_ref, rows_ref.at[z], zs.at[part, at], zr.at[part, z], line_peer(at)).wait_send()
+
+            @pl.when(chosen(at))
+            def _():
+                remote(
+                    own_ref, rows_ref.at[z], zs.at[part, at], zr.at[part, z], line_peer(at)
+                ).wait_send()
 
     t_copies = [
         remote(tab_v.at[0], tab_v.at[YN - k], ts.at[k], tr.at[k], y_peer(k)) for k in range(1, YN)
     ]
 
+    def reaches(at):
+        return jnp.logical_not(beyond & (at == 0))
+
+    half_rows = rows_hi.at[ZN // 2 : ZN]
+    passed = remote(half_rows, half_rows, hs.at[0], hr.at[0], (jnp.where(relay, 0, 1) * YN + y, sub))
+
     def meet_and_send():
-        expected = jnp.where(second, ZN - 1, z) + len(side_peers) * direct.astype(jnp.int32)
+        expected = jnp.where(second, ZN - 1, z - beyond.astype(jnp.int32)) + len(side_peers) * direct.astype(jnp.int32)
         pl.semaphore_wait(barrier, expected + (second & is_end).astype(jnp.int32))
 
         @pl.when(second & is_end)
@@ -264,11 +284,11 @@
             for k in range(1, 8):
                 signal(side_sem, e_peer(k))
 
-        z_start(own_hi, rows_hi, 0, lambda at: second | (at < z))
+        z_start(own_hi, rows_hi, 0, lambda at: second | ((at < z) & reaches(at)))
         for i in range(ZN - 1):
             at = line_at(i)
 
-            @pl.when(first & (at < z))
+            @pl.when(first & (at < z) & reaches(at))
             def _():
                 signal(up_sem, line_peer(at))
 
@@ -285,7 +305,17 @@
     def answer_line():
         @pl.when(z < ZN - 1)
         def _():
-            pl.semaphore_wait(up_sem, ZN - 1 - z)
+            pl.semaphore_wait(up_sem, jnp.where(origin, ZN // 2 - 1, ZN - 1 - z))
+
+        @pl.when(relay)
+        def _():
+            z_wait(own_hi, rows_hi, 0, lambda at: at >= ZN // 2)
+            passed.start()
+
+        @pl.when(origin)
+        def _():
+            z_start(own_hi, rows_hi, 0, lambda at: (at > z) & (at < ZN // 2))
+            passed.wait_recv()
 
         @pl.when(z == 0)
         def _():
@@ -297,7 +327,7 @@
             for peer in side_peers:
                 signal(side_sem, peer)
 
-        z_start(own_hi, rows_hi, 0, lambda at: at > z)
+        z_start(own_hi, rows_hi, 0, lambda at: (at > z) & jnp.logical_not(origin & (at < ZN // 2)))
 
         @pl.when(hub)
         def _():
@@ -426,7 +456,7 @@
             sel_v[t, j * PATCH : (j + 1) * PATCH, :] = jnp.where(hit, 1.0, 0.0).astype(BF16)
 
     loads[3].wait()
-    z_wait(own_hi, rows_hi, 0)
+    z_wait(own_hi, rows_hi, 0, lambda at: jnp.logical_not((relay | origin) & (at >= ZN // 2)))
 
     def pick_row(t, entry, rows):
         wanted = jnp.broadcast_to(tab_v[t, entry : entry + 1, :], (QN, PATCH))
@@ -444,8 +474,6 @@
             copy = remote(fsend.at[t], frecv.at[t], fs.at[t], fr.at[t], y_peer(t))
             copy.start()
             f_copies.append(copy)
-    z_start(own_lo, rows_lo, 1, lambda at: at >= 0)
-
     @pl.when(first & (z == 0))
     def _():
         pl.semaphore_wait(side_sem, 7)
@@ -479,6 +507,7 @@
                     copy = remote(csend, crecv.at[at], cs.at[at], cr.at[at], s_peer(dx, dh, dc))
                     copy.start()
                     c_copies.append(copy)
+    z_start(own_lo, rows_lo, 1, lambda at: at >= 0)
     for copy in c_copies:
         copy.wait_recv()
 
@@ -497,29 +526,20 @@
                 for r in range(1, OWN):
                     value += weights[r] * basis_d[r, at : at + QN, :]
                 psend[hh, xx * 2 + cc] = value
+    psend_b[...] = psend[1 - h].astype(BF16)
     p_copies = [[], []]
-    for g in range(2):
-        half = 1 - h if g == 0 else h
-        for k in range(1, 8):
-            copy = remote(
-                psend.at[half, (s8 + k) % 8],
-                precv.at[g, k],
-                ps.at[g, k],
-                pr.at[g, k],
-                e_peer(k),
-            )
-            copy.start()
-            p_copies[g].append(copy)
-    for copy in p_copies[0]:
-        copy.wait_recv()
-    other = psend[1 - h, s8]
+    for k in (4, 5, 3, 2, 6, 1, 7, 0):
+        at = (s8 + k) % 8
+        peer = (dom, (at // 2) * 4 + (1 - h) * 2 + at % 2)
+        copy = remote(psend_b.at[at], precv_b.at[k], ps.at[0, k], pr.at[0, k], peer)
+        copy.start()
+        p_copies[0].append(copy)
     for k in range(1, 8):
-        other += precv[0, k]
-    hsend[...] = other
-    h_copy = remote(hsend, hrecv, hs.at[0], hr.at[0], across)
-    h_copy.start()
-
-    z_wait(own_lo, rows_lo, 1)
+        copy = remote(psend.at[h, (s8 + k) % 8], precv.at[k], ps.at[1, k], pr.at[1, k], e_peer(k))
+        copy.start()
+        p_copies[1].append(copy)
+
+    z_wait(own_lo, rows_lo, 1, lambda at: at >= 0)
     full_rows = [rows_hi[k].astype(F32) + rows_lo[k].astype(F32) for k in range(ZN)]
     n_copies = []
     for t in (2, 1, 3, 0):
@@ -540,9 +560,12 @@
         copy.wait_recv()
     far = psend[h, s8]
     for k in range(1, 8):
-        far += precv[1, k]
-    h_copy.wait_recv()
-    incoming = near + (far + hrecv[...])
+        far += precv[k]
+    for copy in p_copies[0]:
+        copy.wait_recv()
+    for k in range(8):
+        far += precv_b[k].astype(F32)
+    incoming = near + far
 
     patch_col = sub * COLS + iota((QN, PATCH), 0) * 16 + iota((QN, PATCH), 1) // TROW
     live_trace = patch_col < live
@@ -565,11 +588,15 @@
     ).astype(BF16)
     field_ref[0] = x_v[:, 0:COLS] + dot_nt(g3_v[...], wide)
 
-    z_sent(own_hi, rows_hi, 0)
-    z_sent(own_lo, rows_lo, 1)
+    z_sent(own_hi, rows_hi, 0, reaches)
+
+    @pl.when(relay)
+    def _():
+        passed.wait_send()
+
+    z_sent(own_lo, rows_lo, 1, lambda at: at >= 0)
     for copy in t_copies + f_copies + n_copies + c_copies + p_copies[0] + p_copies[1]:
         copy.wait_send()
-    h_copy.wait_send()
 
 
 def body(*operands):
@@ -613,9 +640,9 @@
             pltpu.VMEM((1, 256), F32),
             pltpu.VMEM((SUB, 1, 256), F32),
             pltpu.VMEM((2, 8) + patches, F32),
-            pltpu.VMEM((2, 8) + patches, F32),
-            pltpu.VMEM(patches, F32),
-            pltpu.VMEM(patches, F32),
+            pltpu.VMEM((8,) + patches, F32),
+            pltpu.VMEM((8,) + patches, BF16),
+            pltpu.VMEM((8,) + patches, BF16),
             pltpu.VMEM(patches, F32),
             pltpu.VMEM((BLK, 3 * PATCH), BF16),
             pltpu.VMEM((PATCH, 3 * PATCH), BF16),

time: 70.7 us -> 68.5 us (0.969)
  Pallas kernels: 67.8 us -> 65.6 us
    pallas_call x1, Pallas kernels: 67.8 us -> 65.6 us  [body(): pl.pallas_call(kernel, out_shape=(jax.ShapeDtypeStruct((1, BLK, COLS), F3...]
where the time goes in v4:
time: 68.5 us; the launch traced here: 68.3 us
  Pallas kernels  65.6 us (96%)
  local copies, waits for them, and re-layouts  1.39 us (2%)
  between operations  1.29 us (2%)
    pallas_call x1, Pallas kernels, body(): pl.pallas_call(kernel, out_shape=(jax.ShapeDtypeStruct((1, BLK, COLS), F3...  65.6 us
    unnamed x2, local copies, waits for them, and re-layouts  1.39 us

profile of v4, /device:TPU:1, one launch (start us, length us, event | category | flops | bytes accessed | tf_op | source)
XLA Modules:
  0.0 68.3 jit_solution(5754790832186348124)
XLA Ops:
  1.3 65.6 %robin_sweep.1 = (f32[1,512,256]{2,1,0:T(8,128)S(1)}, f32[1,2048]{1,0:T(1,128)S(1)}) custom-call(bf16[1,512,256]{2,1,0:T(8,128)(2,1)} %exc_hbm.1, f32[1,512,512]{2,1,0:T(8,128)} %stiff_hbm.1, f32[1,2048]{1,0:T(1,128)} %trace_hbm.1, s32[1,4]{1,0:T(1,128)} %neigh_hbm.1, s32[1,2]{1,0:T(1,128)} %farl_hbm.1, s32[1,4,128]{2,1,0:T(4,128)} %perm_hbm.1, ...), custom_call_target="tpu_custom_call" | custom-call | tf_op jit(solution)/shard_map/robin_sweep/pallas_call | solution.py:607
  66.9 0.8 %copy.14 = f32[1,512,256]{2,1,0:T(8,128)} copy(f32[1,512,256]{2,1,0:T(8,128)S(1)} %get-tuple-element.4) | data formatting | bytes 1048576
  67.7 0.6 copy.15

commit v5 on v4

--- a/solution.py
+++ b/solution.py
@@ -171,6 +171,15 @@
     def signal(sem, peer):
         pl.semaphore_signal(sem, inc=1, device_id=peer, device_id_type=MESH)
 
+    barrier = pltpu.get_barrier_semaphore()
+    side_peers = [y_peer(k) for k in range(1, YN)] + [e_peer(k) for k in range(1, 8)]
+    for i in range(ZN - 1):
+        at = line_at(i)
+
+        @pl.when(second | ((at > z) & jnp.logical_not(origin & (at >= ZN // 2))))
+        def _():
+            signal(barrier, line_peer(at))
+
     smalls = [
         pltpu.make_async_copy(trace_hbm, trace_ref, lsem.at[4]),
         pltpu.make_async_copy(perm_hbm, perm_ref, lsem.at[5]),
@@ -180,15 +189,6 @@
     ]
     for load in smalls:
         load.start()
-
-    barrier = pltpu.get_barrier_semaphore()
-    side_peers = [y_peer(k) for k in range(1, YN)] + [e_peer(k) for k in range(1, 8)]
-    for i in range(ZN - 1):
-        at = line_at(i)
-
-        @pl.when(second | ((at > z) & jnp.logical_not(origin & (at >= ZN // 2))))
-        def _():
-            signal(barrier, line_peer(at))
 
     @pl.when(direct)
     def _():
@@ -553,8 +553,19 @@
             copy.start()
             n_copies.append(copy)
 
+    z_sent(own_hi, rows_hi, 0, reaches)
+
+    @pl.when(relay)
+    def _():
+        passed.wait_send()
+
+    z_sent(own_lo, rows_lo, 1, lambda at: at >= 0)
+    for copy in t_copies + f_copies + c_copies + p_copies[1]:
+        copy.wait_send()
     for copy in n_copies:
         copy.wait_recv()
+    for copy in n_copies:
+        copy.wait_send()
     near = (nsend[0] + nrecv[1]) + (nrecv[2] + nrecv[3])
     for copy in p_copies[1]:
         copy.wait_recv()
@@ -588,14 +599,7 @@
     ).astype(BF16)
     field_ref[0] = x_v[:, 0:COLS] + dot_nt(g3_v[...], wide)
 
-    z_sent(own_hi, rows_hi, 0, reaches)
-
-    @pl.when(relay)
-    def _():
-        passed.wait_send()
-
-    z_sent(own_lo, rows_lo, 1, lambda at: at >= 0)
-    for copy in t_copies + f_copies + n_copies + c_copies + p_copies[0] + p_copies[1]:
+    for copy in p_copies[0]:
         copy.wait_send()
 
 

time: 68.5 us -> 68.4 us (level)
  no operation moved by 1% of the time
where the time goes in v5:
time: 68.4 us; the launch traced here: 68.2 us
  Pallas kernels  65.5 us (96%)
  local copies, waits for them, and re-layouts  1.39 us (2%)
  between operations  1.29 us (2%)
    pallas_call x1, Pallas kernels, body(): pl.pallas_call(kernel, out_shape=(jax.ShapeDtypeStruct((1, BLK, COLS), F3...  65.5 us
    unnamed x2, local copies, waits for them, and re-layouts  1.39 us

profile of v5, /device:TPU:1, one launch (start us, length us, event | category | flops | bytes accessed | tf_op | source)
XLA Modules:
  0.0 68.2 jit_solution(16023963880031560647)
XLA Ops:
  1.3 65.5 %robin_sweep.1 = (f32[1,512,256]{2,1,0:T(8,128)S(1)}, f32[1,2048]{1,0:T(1,128)S(1)}) custom-call(bf16[1,512,256]{2,1,0:T(8,128)(2,1)} %exc_hbm.1, f32[1,512,512]{2,1,0:T(8,128)} %stiff_hbm.1, f32[1,2048]{1,0:T(1,128)} %trace_hbm.1, s32[1,4]{1,0:T(1,128)} %neigh_hbm.1, s32[1,2]{1,0:T(1,128)} %farl_hbm.1, s32[1,4,128]{2,1,0:T(4,128)} %perm_hbm.1, ...), custom_call_target="tpu_custom_call" | custom-call | tf_op jit(solution)/shard_map/robin_sweep/pallas_call | solution.py:611
  66.8 0.8 %copy.14 = f32[1,512,256]{2,1,0:T(8,128)} copy(f32[1,512,256]{2,1,0:T(8,128)S(1)} %get-tuple-element.4) | data formatting | bytes 1048576
  67.6 0.6 copy.15

commit v6 on v4

--- a/solution.py
+++ b/solution.py
@@ -416,8 +416,9 @@
             got = got[0:8] + got[8:16] + got[16:24]
             t0_v[q : q + 1, :] = jnp.sum(jnp.where(keep, got, 0.0), axis=0, keepdims=True)
 
+    sends_first = first | ((z >= ZN // 4) & (z < ZN - ZN // 4))
     def phase(at, carry):
-        @pl.when((at == 0) == first)
+        @pl.when((at == 0) == sends_first)
         def _():
             meet_and_send()
 

time: 68.5 us -> 68.4 us (level)
  no operation moved by 1% of the time
where the time goes in v6:
time: 68.4 us; the launch traced here: 68.3 us
  Pallas kernels  65.6 us (96%)
  local copies, waits for them, and re-layouts  1.39 us (2%)
  between operations  1.29 us (2%)
    pallas_call x1, Pallas kernels, body(): pl.pallas_call(kernel, out_shape=(jax.ShapeDtypeStruct((1, BLK, COLS), F3...  65.6 us
    unnamed x2, local copies, waits for them, and re-layouts  1.39 us

profile of v6, /device:TPU:1, one launch (start us, length us, event | category | flops | bytes accessed | tf_op | source)
XLA Modules:
  0.0 68.3 jit_solution(7325998415293845126)
XLA Ops:
  1.3 65.6 %robin_sweep.1 = (f32[1,512,256]{2,1,0:T(8,128)S(1)}, f32[1,2048]{1,0:T(1,128)S(1)}) custom-call(bf16[1,512,256]{2,1,0:T(8,128)(2,1)} %exc_hbm.1, f32[1,512,512]{2,1,0:T(8,128)} %stiff_hbm.1, f32[1,2048]{1,0:T(1,128)} %trace_hbm.1, s32[1,4]{1,0:T(1,128)} %neigh_hbm.1, s32[1,2]{1,0:T(1,128)} %farl_hbm.1, s32[1,4,128]{2,1,0:T(4,128)} %perm_hbm.1, ...), custom_call_target="tpu_custom_call" | custom-call | tf_op jit(solution)/shard_map/robin_sweep/pallas_call | solution.py:608
  66.9 0.8 %copy.14 = f32[1,512,256]{2,1,0:T(8,128)} copy(f32[1,512,256]{2,1,0:T(8,128)S(1)} %get-tuple-element.4) | data formatting | bytes 1048576
  67.7 0.6 copy.15
